TPU v7x, 256 devices: a whole 4x4x8 slice. The times are simulated.
256 devices in a mesh: seq: 32 (over z_hi, x, core), chan: 8 (over y, z_lo).
Axes of the slice: x: 4, y: 4, z: 8 (z_hi: 4, z_lo: 2; z = z_hi * 2 + z_lo), core: 2. Of those that a mesh axis runs over, the one named last changes fastest.
Arguments:
- tokens: bfloat16 [20480, 8192], P('seq'), may hold values from -6 to 6
- w_query: bfloat16 [8192, 2048], P('seq', 'chan'), may hold values from -0.0625 to 0.0625
- w_keyval: bfloat16 [8192, 2, 2048], P('seq', None, 'chan'), may hold values from -0.0625 to 0.0625
- short_taps: float32 [3, 3, 2048], P(None, None, 'chan'), may hold values from -3 to 3
- skip_gain: float32 [2048], P('chan'), may hold values from -4 to 4
- decay_rates: float32 [2048, 16], P('chan'), may hold values from 2.4414063e-05 to 0.06
- residues: float32 [2048, 16], P('chan'), may hold values from -0.2 to 0.2
- w_output: bfloat16 [2048, 8192], P('seq', 'chan'), may hold values from -0.125 to 0.125
Outputs:
- mixed: bfloat16 [20480, 8192], P('seq', 'chan')
All inputs are finite; a program needn't handle non-finite values.
Results may differ from a plain program's by a relative error of at most 0.0049.
Values may be sent and summed in bfloat16 or wider, within the bound.
A program may use at most 128 MiB of HBM per device.

v0:
```python
import jax
import jax.numpy as jnp
import numpy as np
from jax import lax
from jax.sharding import PartitionSpec as P


def shifted(value, axis, steps):
    count = lax.axis_size(axis)
    initial, last = (max(0, -steps), min(count, count - steps))
    return lax.ppermute(value, axis, [(source, source + steps) for source in range(initial, last)])


def modal_block(signal, rates, weights):
    group, length = signal.shape
    span = min(128, length)
    blocks = length // span
    offsets = jnp.arange(span, dtype=jnp.float32)
    highest = lax.Precision.HIGHEST
    decays = jnp.exp(-rates[:, :, None] * offsets)
    impulse = jnp.einsum("gm,gms->gs", weights, decays, precision=highest)
    lagged = np.arange(span)[:, None] - np.arange(span)[None, :]
    toeplitz = jnp.where(lagged >= 0, impulse[:, np.maximum(lagged, 0)], 0.0)
    pieces = signal.reshape(group, blocks, span)
    inner = jnp.einsum("gij,gbj->gbi", toeplitz, pieces, precision=highest)
    tail_decay = jnp.exp(-rates[:, :, None] * (span - 1.0 - offsets))
    block_end = jnp.einsum("gmj,gbj->gbm", tail_decay, pieces, precision=highest)
    counter = np.arange(blocks)
    spacing = counter[:, None] - 1 - counter[None, :]
    distance = (np.maximum(spacing, 0) * span).astype(np.float32)
    hops = jnp.where(spacing >= 0, jnp.exp(-rates[:, :, None, None] * distance), 0.0)
    entering = jnp.einsum("gmbk,gkm->gbm", hops, block_end, precision=highest)
    leading = weights[:, :, None] * jnp.exp(-rates[:, :, None] * (offsets + 1.0))
    output = inner + jnp.einsum("gmi,gbm->gbi", leading, entering, precision=highest)
    final = jnp.exp(-rates * span) * entering[:, -1] + block_end[:, -1]
    return (output.reshape(group, length), final)


def grouped_conv(signal, rates, weights):
    width, length = signal.shape
    group = min(16, width)
    count = width // group
    modes = rates.shape[1]

    def single(pieces):
        return modal_block(pieces[0], pieces[1], pieces[2])

    outputs, finals = lax.map(
        single,
        (
            signal.reshape(count, group, length),
            rates.reshape(count, group, modes),
            weights.reshape(count, group, modes),
        ),
    )
    return (outputs.reshape(width, length), finals.reshape(width, modes))


def long_conv(mixed_kv, decay_rates, residues):
    spread = lax.all_to_all(mixed_kv, "seq", split_axis=0, concat_axis=1, tiled=True)
    width = spread.shape[0]
    offset = lax.axis_index("seq") * width
    mine_rates = lax.dynamic_slice_in_dim(decay_rates, offset, width, 0)
    mine_weights = lax.dynamic_slice_in_dim(residues, offset, width, 0)
    result, ignored = grouped_conv(spread, mine_rates, mine_weights)
    return lax.all_to_all(result, "seq", split_axis=1, concat_axis=0, tiled=True)


def featurize(projected, weights, before):
    extended = jnp.concatenate([before, projected], axis=2)
    return (
        weights[0][:, :, None] * extended[:, :, 2:]
        + weights[1][:, :, None] * extended[:, :, 1:-1]
        + weights[2][:, :, None] * extended[:, :, :-2]
    )


def shards(tokens, w_query, w_keyval, short_taps, skip_gain, decay_rates, residues, w_output):

    def add_projection(portion):
        return jnp.einsum("dpc,td->pct", portion, tokens, preferred_element_type=jnp.float32)

    stacked = jnp.concatenate(
        [
            add_projection(lax.all_gather(w_query[:, None, :], "seq", axis=0, tiled=True)),
            add_projection(lax.all_gather(w_keyval, "seq", axis=0, tiled=True)),
        ],
        axis=0,
    )
    before = shifted(stacked[:, :, -2:], "seq", 1)
    featured = featurize(stacked, short_taps, before)
    query_feat = featured[0]
    mixed_kv = featured[1] * featured[2]
    convolved = long_conv(mixed_kv, decay_rates, residues)
    summed = convolved + skip_gain[:, None] * mixed_kv
    gated_feat = (query_feat * summed).astype(jnp.bfloat16)
    everyone = lax.all_gather(gated_feat, "chan", axis=0, tiled=True)
    result = lax.dot_general(
        everyone,
        lax.all_gather(w_output, "seq", axis=0, tiled=True),
        (((0,), (0,)), ((), ())),
        preferred_element_type=jnp.float32,
    )
    return result.astype(jnp.bfloat16)


def solution(mesh):
    return jax.shard_map(
        shards,
        mesh=mesh,
        in_specs=(
            P("seq", None),
            P("seq", "chan"),
            P("seq", None, "chan"),
            P(None, None, "chan"),
            P("chan"),
            P("chan", None),
            P("chan", None),
            P("seq", "chan"),
        ),
        out_specs=P("seq", "chan"),
        check_vma=False,
    )
```

profile of v0, /device:TPU:1, one launch (start us, length us, event | category | flops | bytes accessed | tf_op | source)
XLA Modules:
  0.0 391.2 jit_solution(24873833520991337)
XLA Ops:
  6.5 0.0 all-gather.12.cloned.1.call-start
  6.5 0.7 all-gather.12.cloned.1.call-update
  7.3 0.0 all-gather.6.cloned.1.call-start
  7.3 1.8 copy.21
  9.1 0.0 all-gather.6.cloned.1.call-update
  9.1 0.0 all-gather.10.cloned.1.call-start
  9.2 0.7 all-gather.10.cloned.1.call-update
  9.9 64.7 %all-gather.12.cloned.1.call-done = bf16[8192,256]{1,0:T(8,128)(2,1)} async-done(((bf16[256,256]{1,0:T(8,128)(2,1)}), bf16[8192,256]{1,0:T(8,128)(2,1)}) %all-gather.12.cloned.1.call-update) | async-done | bytes 4194320 | tf_op jit(solution)/shard_map/all_gather | solution.py:85
  74.6 11.3 %convolution_bitcast_fusion = f32[1,256,640]{2,1,0:T(8,128)S(1)} fusion(bf16[8192,256]{1,0:T(8,128)(2,1)} %all-gather.12.cloned.1.call-done, bf16[640,8192]{1,0:T(8,128)(2,1)} %param.13), kind=kOutput, calls=%fused_computation.21 | convolution fusion | flops 2684354560 | bytes 15335424 | tf_op jit(solution)/shard_map/dpc,td->pct/dot_general | solution.py:81
  85.9 0.0 copy-start.3
  85.9 74.3 %all-gather.6.cloned.1.call-done = bf16[8192,2,256]{0,2,1:T(8,128)(2,1)} async-done(((bf16[256,2,256]{0,2,1:T(8,128)(2,1)}), bf16[8192,2,256]{0,2,1:T(8,128)(2,1)}) %all-gather.6.cloned.1.call-update) | async-done | bytes 8388624 | tf_op jit(solution)/shard_map/all_gather | solution.py:86
  160.2 14.9 %fusion.4 = f32[2,256,640]{2,1,0:T(8,128)S(1)} fusion(bf16[8192,2,256]{0,2,1:T(8,128)(2,1)} %all-gather.6.cloned.1.call-done, bf16[640,8192]{1,0:T(8,128)(2,1)} %param.13), kind=kOutput, calls=%fused_computation.5 | convolution fusion | flops 5368709120 | bytes 20185088 | tf_op jit(solution)/shard_map/dpc,td->pct/dot_general | solution.py:81
  175.2 0.2 fusion.18
  175.3 2.9 collective-permute-start
  178.3 0.0 copy-done.3
  178.3 5.5 %collective-permute-done = f32[3,256,2]{2,1,0:T(8,128)S(1)} collective-permute-done((f32[3,256,2]{2,1,0:T(8,128)S(1)}, f32[3,256,2]{2,1,0:T(8,128)S(1)}, u32[]{:S(2)}, u32[]{:S(2)}) %collective-permute-start) | collective-permute-done | bytes 6176 | tf_op jit(solution)/shard_map/ppermute | solution.py:11
  183.7 0.7 maximum_maximum_fusion
  184.4 1.1 fusion.12
  185.5 0.0 copy-start.4
  185.5 0.0 copy-start.5
  185.6 0.0 copy-start
  185.6 0.9 fusion.21
  186.5 13.7 %all-to-all-start = ((f32[32,8,640]{2,1,0:T(8,128)}), f32[32,8,640]{2,1,0:T(8,128)S(1)}, u32[]{:S(2)}, u32[]{:S(2)}) async-start(f32[32,8,640]{2,1,0:T(8,128)} %fusion.21), calls=%async_computation | async-start | bytes 1310720 | tf_op jit(solution)/shard_map/all_to_all | solution.py:60
  200.2 0.0 all-gather.8.cloned.1.call-start
  200.2 0.0 copy-done.4
  200.2 0.0 copy-done.5
  200.3 0.1 constant_dynamic-slice_fusion
  200.3 0.1 copy.34
  200.4 0.1 copy.33
  200.5 0.1 multiply_reduce_fusion
  200.6 0.1 copy.30
  200.7 0.0 copy-done
  200.7 54.5 %gather_fusion = f32[16384,8]{1,0:T(8,128)} fusion(f32[8,128]{0,1:T(8,128)S(1)} %copy.30, s32[16384]{0:T(1024)S(1)} %broadcast_clamp_fusion), kind=kCustom, calls=%fused_computation | custom fusion | bytes 1114112 | tf_op jit(solution)/shard_map/while/body/eval_jaxpr/gather | solution.py:23
  255.2 0.0 copy-start.1
  255.2 5.9 %copy.24 = f32[128,128,8]{1,0,2:T(8,128)} copy(f32[128,128,8]{2,1,0:T(8,128)} %bitcast.48) | data formatting | bytes 1048576 | tf_op jit(solution)/shard_map/while/body/eval_jaxpr/gather | solution.py:23
  261.1 0.0 copy-done.1
  261.1 0.0 copy-start.2
  261.2 0.0 all-to-all-done
  261.2 0.1 copy.22
  261.4 0.7 convolution_bitcast_fusion.1
  262.1 0.3 copy.31
  262.4 0.0 copy-done.2
  262.4 2.2 fusion.15
  264.6 20.1 %fusion = f32[8,16,1,160]{3,2,1,0:T(1,128)S(1)} fusion(f32[8,160,16,1]{1,3,2,0:T(1,128)S(1)} %copy.31, f32[160,160]{1,0:T(8,128)} %constant.49.clone, f32[8,16]{1,0:T(8,128)S(1)} %neg.10, pred[160,160]{1,0:T(8,128)(4,1)S(1)} %copy.39), kind=kOutput, calls=%fused_computation.1 | convolution fusion | flops 45875200 | bytes 292352 | tf_op jit(solution)/shard_map/while/body/eval_jaxpr/gmbk,gkm->gbm/dot_general | solution.py:32
  284.7 0.0 copy-start.6
  284.7 1.3 convolution_add_fusion
  286.0 0.1 all_to_all.26
  286.2 0.4 copy.26
  286.6 28.3 %all_to_all.32 = f32[8,32,640]{2,0,1:T(8,128)S(1)} all-to-all(f32[8,32,640]{2,0,1:T(8,128)S(1)} %copy.26), channel_id=1, replica_groups=mesh['seq'=32,'chan'=8] {'seq'}, dimensions={1} | all-to-all | bytes 1310720 | tf_op jit(solution)/shard_map/all_to_all | solution.py:66
  314.9 0.0 copy-done.6
  314.9 0.9 fusion.14
  315.8 0.0 all-gather.8.cloned.1.call-update
  315.9 0.0 all-gather.10.cloned.1.call-done
  315.9 61.8 %all-gather.8.cloned.1.call-done = bf16[2048,640]{1,0:T(8,128)(2,1)} async-done(((bf16[256,640]{1,0:T(8,128)(2,1)}), bf16[2048,640]{1,0:T(8,128)(2,1)}) %all-gather.8.cloned.1.call-update) | async-done | bytes 2621456 | tf_op jit(solution)/shard_map/all_gather | solution.py:97
  377.7 7.0 %convolution_convert_fusion = bf16[640,1024]{1,0:T(8,128)(2,1)} fusion(bf16[2048,640]{1,0:T(8,128)(2,1)} %all-gather.8.cloned.1.call-done, bf16[2048,1024]{1,0:T(8,128)(2,1)} %all-gather.10.cloned.1.call-done), kind=kOutput, calls=%fused_computation.20 | convolution fusion | flops 2685009920 | bytes 8126464 | tf_op jit(solution)/shard_map/dot_general | solution.py:98
  (7 shorter events, 0.1 us)
Async XLA Ops:
  6.5 68.1 %all-gather.12.cloned.1.call-start = ((), (), s32[]{:S(2)}) async-start(), calls=%async_computation.5 | async-start | bytes 4325376 | tf_op jit(solution)/shard_map/all_gather | solution.py:85
  7.3 153.0 %all-gather.6.cloned.1.call-start = ((), (), s32[]{:S(2)}) async-start(), calls=%async_computation.2 | async-start | bytes 8650752 | tf_op jit(solution)/shard_map/all_gather | solution.py:86
  9.1 306.7 %all-gather.10.cloned.1.call-start = ((), (), s32[]{:S(2)}) async-start(), calls=%async_computation.4 | async-start | bytes 4325376 | tf_op jit(solution)/shard_map/all_gather | solution.py:100
  85.9 92.3 %copy-start.3 = (f32[3,3,256]{2,1,0:T(4,128)S(1)}, f32[3,3,256]{2,1,0:T(4,128)}, u32[]{:S(2)}) copy-start(f32[3,3,256]{2,1,0:T(4,128)} %param.16) | copy-start | bytes 27652
  175.3 8.4 %collective-permute-start = (f32[3,256,2]{2,1,0:T(8,128)S(1)}, f32[3,256,2]{2,1,0:T(8,128)S(1)}, u32[]{:S(2)}, u32[]{:S(2)}) collective-permute-start(f32[3,256,2]{2,1,0:T(8,128)S(1)} %fusion.18), channel_id=1, source_target_pairs={{0,8},{8,16},{16,24},{24,32},{32,40},{40,48},{48,56},{56,64},{64,7... | collective-permute-start | bytes 18440 | tf_op jit(solution)/shard_map/ppermute | solution.py:11
  185.5 14.7 %copy-start.4 = (f32[256,16]{0,1:T(8,128)S(1)}, f32[256,16]{0,1:T(8,128)}, u32[]{:S(2)}) copy-start(f32[256,16]{0,1:T(8,128)} %param.18) | copy-start | bytes 49156
  185.5 14.7 %copy-start.5 = (f32[256,16]{0,1:T(8,128)S(1)}, f32[256,16]{0,1:T(8,128)}, u32[]{:S(2)}) copy-start(f32[256,16]{0,1:T(8,128)} %param.19) | copy-start | bytes 49156
  185.6 15.2 %copy-start = (s32[16384]{0:T(1024)S(1)}, s32[16384]{0:T(1024)}, u32[]{:S(2)}) copy-start(s32[16384]{0:T(1024)} %constant.52) | copy-start | bytes 196612
  186.5 74.7 %all-to-all-start = ((f32[32,8,640]{2,1,0:T(8,128)}), f32[32,8,640]{2,1,0:T(8,128)S(1)}, u32[]{:S(2)}, u32[]{:S(2)}) async-start(f32[32,8,640]{2,1,0:T(8,128)} %fusion.21), calls=%async_computation | async-start | bytes 1310720 | tf_op jit(solution)/shard_map/all_to_all | solution.py:60
  200.2 177.5 %all-gather.8.cloned.1.call-start = ((), (), s32[]{:S(2)}) async-start(), calls=%async_computation.3 | async-start | bytes 2949120 | tf_op jit(solution)/shard_map/all_gather | solution.py:97
  255.2 5.9 %copy-start.1 = (pred[160,160]{1,0:T(32,128)(4,1)S(1)}, pred[160,160]{1,0:T(32,128)(4,1)}, u32[]{:S(2)}) copy-start(pred[160,160]{1,0:T(32,128)(4,1)} %constant.50.clone) | copy-start | bytes 76804
  261.1 1.3 copy-start.2
  284.7 30.2 %copy-start.6 = (f32[256]{0:T(256)S(1)}, f32[256]{0:T(256)}, u32[]{:S(2)}) copy-start(f32[256]{0:T(256)} %param.17) | copy-start | bytes 3076
Sparse Core Ops, SparseCore 0:
  9.9 64.6 all-gather.11
  77.1 83.0 all-gather.5
  162.8 72.8 all-gather.9
  316.0 61.6 all-gather.7
where the time goes:
time: 392 us; the launch traced here: 391 us
  waiting for transfers between devices  208 us (53%)
  local copies, waits for them, and re-layouts  63.6 us (16%)
  matrix products  57.6 us (15%)
  blocking collectives  28.3 us (7%)
  starting transfers between devices  16.7 us (4%)
  between operations  13.3 us (3%)
    all_gather x1, waiting for transfers between devices, shards(): lax.all_gather(w_keyval, 'seq', axis=0, tiled=True)  74.3 us
    all_gather x1, waiting for transfers between devices, shards(): lax.all_gather(w_query[:, None, :], 'seq', axis=0, tiled=True)  64.7 us
    all_gather x1, waiting for transfers between devices, shards(): everyone = lax.all_gather(gated_feat, 'chan', axis=0, tiled=True)  61.8 us
    gather x2, local copies, waits for them, and re-layouts, modal_block(): toeplitz = jnp.where(lagged >= 0, impulse[:, np.maximum(lagged, 0)], 0.0)  60.4 us
    all_to_all x1, blocking collectives, long_conv(): lax.all_to_all(result, 'seq', split_axis=1, concat_axis=0, tiled=True)  28.3 us
    dot_general x2, matrix products, add_projection(): jnp.einsum('dpc,td->pct', portion, tokens, preferred_element_type=jnp.flo...  26.3 us
    dot_general x1, matrix products, modal_block(): entering = jnp.einsum('gmbk,gkm->gbm', hops, block_end, precision=highest)  20.1 us
    all_to_all x1, starting transfers between devices, long_conv(): lax.all_to_all(mixed_kv, 'seq', split_axis=0, concat_axis=1, tiled=True)  13.7 us
  transfers between devices with their start and end apart: 6, of which 4 were waited for; matrix products, arithmetic and copies ran while one was open for 30% of the time, Pallas kernels for 0%

commit v1 on v0

v1 whole, which is shorter than its diff:
```python
import functools

import jax
import jax.numpy as jnp
from jax import lax
from jax.experimental import pallas as pl
from jax.experimental.pallas import tpu as pltpu
from jax.sharding import PartitionSpec as P

MESH = pl.DeviceIdType.MESH
F32 = jnp.float32
BF16 = jnp.bfloat16
MODES = 16
ROWS = 640
SUB = ROWS // 8
HEAD = 16
NSEM = 36


def wrap(value, count):
    return lax.rem(value, count)


def near(j):
    return lax.rem((j * (j + 1)) // 2, 4)


def kernel(tok, wkv_in, wq_in, wo_in, taps, skip, rates, resid, out,
           x_all, wkv, wq, wo, acc_kv, acc_q, mkv, conv, scan, e_own, e_sib, c_x, r_z, gate,
           send, recv, esend, erecv, gsend, grecv, lsem, tsem):
    seq, chan = lax.axis_index("seq"), lax.axis_index("chan")
    core, xx, zh = lax.rem(seq, 2), lax.rem(seq // 2, 4), seq // 8
    yy, zl = chan // 2, lax.rem(chan, 2)

    def at(z, x, k):
        return (wrap(z, 4) * 4 + wrap(x, 4)) * 2 + k

    def cat(y, l):
        return wrap(y, 4) * 2 + l

    sib = at(zh, xx, 1 - core)
    xp, xm, xo = at(zh, xx + 1, core), at(zh, xx + 3, core), at(zh, xx + 2, core)
    zp, zm, zo = at(zh + 1, xx, core), at(zh + 3, xx, core), at(zh + 2, xx, core)
    yp, ym, lp = cat(yy + 1, zl), cat(yy + 3, zl), cat(yy, 1 - zl)
    following, before = wrap(seq + 1, 32), wrap(seq + 31, 32)

    def copy(src, dst, s, r, **to):
        return pltpu.make_async_remote_copy(
            src_ref=src, dst_ref=dst, send_sem=s, recv_sem=r, device_id=to, device_id_type=MESH)

    barrier = pltpu.get_barrier_semaphore()
    for to in (sib, xp, xm, xo, zp, zm, zo, before):
        pl.semaphore_signal(barrier, inc=1, device_id={"seq": to}, device_id_type=MESH)
    for to in (yp, ym, lp):
        pl.semaphore_signal(barrier, inc=1, device_id={"chan": to}, device_id_type=MESH)
    load = pltpu.make_async_copy(tok, x_all.at[pl.ds(HEAD, ROWS), :], lsem.at[0])
    load.start()
    pl.semaphore_wait(barrier, 11)

    class Gather:
        def __init__(self, p, src, buf, by_rows):
            self.p, self.src, self.buf, self.by_rows = p, src, buf, by_rows
            self.r, self.n = src.shape

        def piece(self, z, x, k, half=None):
            first = pl.multiple_of(at(z, x, k) * self.r, self.r)
            if half is None:
                return self.buf.at[pl.ds(first, self.r), :]
            if self.by_rows:
                h = self.r // 2
                return self.buf.at[pl.ds(pl.multiple_of(first + half * h, h), h), :]
            h = self.n // 2
            return self.buf.at[pl.ds(first, self.r), pl.ds(half * h, h)]

        def put(self, ref, i, to, src=None):
            copy(ref if src is None else src, ref, send.at[self.p, i], recv.at[self.p, i], seq=to).start()

        def got(self, ref, i):
            copy(ref, ref, send.at[self.p, i], recv.at[self.p, i], seq=sib).wait_recv()

        def start(self):
            own = self.piece(zh, xx, core)
            self.local = pltpu.make_async_copy(self.src, own, lsem.at[1 + self.p])
            self.put(own, 0, zp, self.src)
            self.put(own, 1, zm, self.src)
            self.put(own, 4, xp, self.src)
            self.put(own, 8, xm, self.src)
            self.put(own, 20, sib, self.src)
            self.local.start()

        def spread(self, ref, j):
            self.put(ref, 4 + j, xp)
            self.put(ref, 8 + j, xm)
            self.put(ref, 20 + j, sib)

        def z_near(self):
            ref = self.piece(zh + 3, xx, core)
            self.got(ref, 0)
            self.put(self.piece(zh + 3, xx, core, 0), 2, zp)
            self.spread(ref, 2)
            ref = self.piece(zh + 1, xx, core)
            self.got(ref, 1)
            self.put(self.piece(zh + 1, xx, core, 1), 3, zm)
            self.spread(ref, 1)

        def z_far(self):
            self.got(self.piece(zh + 2, xx, core, 0), 2)
            self.got(self.piece(zh + 2, xx, core, 1), 3)
            self.spread(self.piece(zh + 2, xx, core), 3)

        def x_near(self, j):
            z = zh + near(j)
            ref = self.piece(z, xx + 3, core)
            self.got(ref, 4 + j)
            self.put(self.piece(z, xx + 3, core, 0), 12 + j, xp)
            self.put(ref, 24 + j, sib)
            ref = self.piece(z, xx + 1, core)
            self.got(ref, 8 + j)
            self.put(self.piece(z, xx + 1, core, 1), 16 + j, xm)
            self.put(ref, 28 + j, sib)

        def x_far(self, j):
            z = zh + near(j)
            self.got(self.piece(z, xx + 2, core, 0), 12 + j)
            self.got(self.piece(z, xx + 2, core, 1), 16 + j)
            self.put(self.piece(z, xx + 2, core), 32 + j, sib)

        def other(self, j, dx, c):
            z = zh + near(j)
            self.got(self.piece(z, xx + dx, 1 - core), c + j)

        def drain(self):
            full, half = self.piece(zh, xx, core), self.piece(zh, xx, core, 0)

            def sent(ref, i):
                copy(ref, ref, send.at[self.p, i], recv.at[self.p, i], seq=sib).wait_send()

            for i in (0, 1):
                sent(full, i)
            for i in (2, 3):
                sent(half, i)

            @pl.loop(0, 8)
            def _(i):
                sent(full, 4 + i)
                sent(half, 12 + i)
                sent(full, 20 + i)
                sent(full, 28 + i)

    kv = Gather(0, wkv_in, wkv, True)
    qq = Gather(1, wq_in, wq, True)
    ww = Gather(2, wo_in, wo, False)

    def multiply(g, acc, j, dx, c):
        g.other(j, dx, c)
        first = pl.multiple_of(at(zh + near(j), xx + dx, 0) * g.r, 2 * g.r)
        columns = pl.ds(first, 2 * g.r)
        for n in range(g.n // 256):
            acc[:, n * 256:(n + 1) * 256] += jnp.dot(
                x_all[:, columns], g.buf[columns, n * 256:(n + 1) * 256], preferred_element_type=F32)

    def short(acc, cols, which, lanes, i):
        v = acc[pl.ds(pl.multiple_of(i * SUB + HEAD - 8, 8), SUB + 8), cols]
        return (taps[0, which:which + 1, lanes] * v[8:] + taps[1, which:which + 1, lanes] * v[7:-1]
                + taps[2, which:which + 1, lanes] * v[6:-2])

    rank8 = lax.broadcasted_iota(jnp.int32, (8, 128), 0)

    def wide(row):
        return jnp.broadcast_to(row, (8, 128))

    kv.start()
    tail = copy(tok.at[pl.ds(ROWS - HEAD, HEAD), :], x_all.at[pl.ds(0, HEAD), :], tsem.at[0], tsem.at[1], seq=following)
    tail.start()
    acc_kv[...] = jnp.zeros_like(acc_kv)
    acc_q[...] = jnp.zeros_like(acc_q)
    kv.z_near()
    kv.z_far()
    load.wait()
    tail.wait_recv()
    kv.local.wait()

    @pl.loop(0, 4)
    def _(j):
        kv.x_near(j)
        multiply(kv, acc_kv, j, 0, 20)

    qq.start()

    @pl.loop(0, 4)
    def _(j):
        kv.x_far(j)
        multiply(kv, acc_kv, j, 3, 24)
        multiply(kv, acc_kv, j, 1, 28)

    qq.z_near()
    qq.z_far()
    qq.local.wait()

    @pl.loop(0, 4)
    def _(j):
        multiply(kv, acc_kv, j, 2, 32)

    acc_kv[0:HEAD, :] = jnp.where(seq == 0, 0.0, acc_kv[0:HEAD, :])

    for l in range(2):
        lanes = slice(l * 128, (l + 1) * 128)

        @pl.loop(0, 8)
        def _(i):
            key = short(acc_kv, slice(l * 128, (l + 1) * 128), 1, lanes, i)
            value = short(acc_kv, slice(256 + l * 128, 256 + (l + 1) * 128), 2, lanes, i)
            mkv[pl.ds(pl.multiple_of(l * ROWS + i * SUB, 8), SUB), :] = key * value

    for l in range(2):
        lanes = slice(l * 128, (l + 1) * 128)
        a = [wide(jnp.exp(-rates[m:m + 1, lanes])) for m in range(MODES)]
        r = [wide(resid[m:m + 1, lanes]) for m in range(MODES)]

        def step(t, hs):
            v = mkv[pl.ds(l * ROWS + t, 8, stride=SUB), :]
            hs = [a[m] * hs[m] + v for m in range(MODES)]
            terms = [r[m] * hs[m] for m in range(MODES)]
            while len(terms) > 1:
                terms = [p + q for p, q in zip(terms[::2], terms[1::2])]
            conv[pl.ds(l * ROWS + t, 8, stride=SUB), :] = terms[0]
            return tuple(hs)

        hs = lax.fori_loop(0, SUB, step, (jnp.zeros((8, 128), F32),) * MODES)
        for m in range(MODES):
            v = hs[m]
            for d in (1, 2, 4):
                factor = wide(jnp.exp(-rates[m:m + 1, lanes] * float(SUB * d)))
                v = v + jnp.where(rank8 >= d, factor * pltpu.roll(v, d, 0), 0.0)
            scan[l * MODES + m] = v
            e_own[m:m + 1, lanes] = v[7:8, :]

    def eput(src, dst, i, to):
        copy(src, dst, esend.at[i], erecv.at[i], seq=to).start()

    def egot(ref, i):
        copy(ref, ref, esend.at[i], erecv.at[i], seq=sib).wait_recv()

    eput(e_own, e_sib, 0, sib)

    @pl.loop(0, 4)
    def _(j):
        qq.x_near(j)
        multiply(qq, acc_q, j, 0, 20)

    egot(e_sib, 0)
    lam = rates[...]
    e0 = jnp.where(core == 0, e_own[...], e_sib[...])
    e1 = jnp.where(core == 0, e_sib[...], e_own[...])
    step1 = jnp.exp(-lam * float(ROWS))
    c_x[xx] = step1 * e0 + e1
    eput(c_x.at[xx], c_x.at[xx], 1, xp)
    eput(c_x.at[xx], c_x.at[xx], 2, xo)
    eput(c_x.at[xx], c_x.at[xx], 3, xm)
    ww.start()

    @pl.loop(0, 2)
    def _(j):
        qq.x_far(j)
        multiply(qq, acc_q, j, 3, 24)
        multiply(qq, acc_q, j, 1, 28)

    for d in (1, 2, 3):
        egot(c_x.at[wrap(xx + 4 - d, 4)], d)
    row = c_x[3]
    in_chip = jnp.zeros_like(lam)
    for k in range(4):
        if k < 3:
            row = row + jnp.exp(-lam * float(2 * ROWS * (3 - k))) * c_x[k]
            gap = jnp.maximum(xx - 1 - k, 0).astype(F32) * float(2 * ROWS)
            in_chip = in_chip + jnp.where(k < xx, jnp.exp(-lam * gap) * c_x[k], 0.0)
    r_z[zh] = row
    eput(r_z.at[zh], r_z.at[zh], 4, zp)
    eput(r_z.at[zh], r_z.at[zh], 5, zo)
    eput(r_z.at[zh], r_z.at[zh], 6, zm)
    ww.z_near()

    @pl.loop(2, 4)
    def _(j):
        qq.x_far(j)
        multiply(qq, acc_q, j, 3, 24)
        multiply(qq, acc_q, j, 1, 28)

    ww.z_far()
    for d in (1, 2, 3):
        egot(r_z.at[wrap(zh + 4 - d, 4)], 3 + d)
    in_row = jnp.zeros_like(lam)
    for k in range(3):
        gap = jnp.maximum(zh - 1 - k, 0).astype(F32) * float(8 * ROWS)
        in_row = in_row + jnp.where(k < zh, jnp.exp(-lam * gap) * r_z[k], 0.0)
    in_chip = in_chip + jnp.exp(-lam * (xx.astype(F32) * float(2 * ROWS))) * in_row
    enter = jnp.where(core == 0, in_chip, e0 + step1 * in_chip)

    for l in range(2):
        lanes = slice(l * 128, (l + 1) * 128)
        a = [wide(jnp.exp(-rates[m:m + 1, lanes])) for m in range(MODES)]
        gs = []
        for m in range(MODES):
            rate = wide(rates[m:m + 1, lanes])
            first = jnp.where(rank8 >= 1, pltpu.roll(scan[l * MODES + m], 1, 0), 0.0)
            first = first + jnp.exp(-rate * (rank8.astype(F32) * float(SUB))) * wide(enter[m:m + 1, lanes])
            gs.append(wide(resid[m:m + 1, lanes]) * a[m] * first)
        direct = wide(skip[0:1, lanes])

        def step(t, gs):
            terms = list(gs)
            while len(terms) > 1:
                terms = [p + q for p, q in zip(terms[::2], terms[1::2])]
            place = pl.ds(l * ROWS + t, 8, stride=SUB)
            conv[place, :] = conv[place, :] + terms[0] + direct * mkv[place, :]
            return tuple(a[m] * gs[m] for m in range(MODES))

        lax.fori_loop(0, SUB, step, tuple(gs))

    @pl.loop(0, 2)
    def _(j):
        ww.x_near(j)

    @pl.loop(0, 4)
    def _(j):
        multiply(qq, acc_q, j, 2, 32)

    acc_q[0:HEAD, :] = jnp.where(seq == 0, 0.0, acc_q[0:HEAD, :])

    def gref(c, l, half=None):
        ref = gate.at[c * 2 + l]
        return ref if half is None else ref.at[pl.ds(half * (ROWS // 2), ROWS // 2), :]

    def gput(ref, i, l, to):
        copy(ref, ref, gsend.at[l, i], grecv.at[l, i], chan=to).start()

    def ggot(ref, i, l):
        copy(ref, ref, gsend.at[l, i], grecv.at[l, i], chan=lp).wait_recv()

    for l in range(2):
        lanes = slice(l * 128, (l + 1) * 128)
        mine = gate.at[chan * 2 + l]

        @pl.loop(0, 8)
        def _(i):
            query = short(acc_q, lanes, 0, lanes, i)
            done = query * conv[pl.ds(pl.multiple_of(l * ROWS + i * SUB, 8), SUB), :]
            mine[pl.ds(pl.multiple_of(i * SUB, 16), SUB), :] = done.astype(BF16)

        gput(mine, 0, l, lp)
        gput(mine, 1, l, yp)
        gput(mine, 2, l, ym)

    @pl.loop(2, 4)
    def _(j):
        ww.x_near(j)

    for l in range(2):
        ref = gref(lp, l)
        ggot(ref, 0, l)
        gput(ref, 3, l, yp)
        gput(ref, 4, l, ym)

    for l in range(2):
        for j in range(2):
            side = zl if j == 0 else 1 - zl
            ggot(gref(cat(yy + 3, side), l), 1 + 2 * j, l)
            gput(gref(cat(yy + 3, side), l, 0), 5 + 2 * j, l, yp)
            ggot(gref(cat(yy + 1, side), l), 2 + 2 * j, l)
            gput(gref(cat(yy + 1, side), l, 1), 6 + 2 * j, l, ym)

    @pl.loop(0, 4)
    def _(j):
        ww.x_far(j)

    @pl.loop(0, 4)
    def _(j):
        ww.other(j, 0, 20)
        ww.other(j, 3, 24)
        ww.other(j, 1, 28)
        ww.other(j, 2, 32)

    for l in range(2):
        for j in range(2):
            side = zl if j == 0 else 1 - zl
            ggot(gref(cat(yy + 2, side), l, 0), 5 + 2 * j, l)
            ggot(gref(cat(yy + 2, side), l, 1), 6 + 2 * j, l)
    ww.local.wait()

    @pl.loop(0, out.shape[1] // 256)
    def _(n):
        columns = pl.ds(pl.multiple_of(n * 256, 256), 256)
        whole = jnp.concatenate([gate[i] for i in range(16)], axis=1)
        out[:, columns] = jnp.dot(whole, wo[:, columns], preferred_element_type=F32).astype(BF16)

    for g in (kv, qq, ww):
        g.drain()
    tail.wait_send()
    for i, ref in enumerate([e_own] + [c_x.at[0]] * 3 + [r_z.at[0]] * 3):
        copy(ref, ref, esend.at[i], erecv.at[i], seq=sib).wait_send()
    for l in range(2):
        for i in range(9):
            ref = gref(chan, l, None if i < 5 else 0)
            copy(ref, ref, gsend.at[l, i], grecv.at[l, i], chan=lp).wait_send()


def shards(tokens, w_query, w_keyval, short_taps, skip_gain, decay_rates, residues, w_output):
    depth, _, width = w_keyval.shape
    hbm, vmem = pl.BlockSpec(memory_space=pl.ANY), pl.BlockSpec(memory_space=pltpu.VMEM)
    dma = pltpu.SemaphoreType.DMA
    model = tokens.shape[1]
    return pl.pallas_call(
        kernel,
        out_shape=jax.ShapeDtypeStruct((ROWS, w_output.shape[1]), BF16),
        in_specs=[hbm] * 4 + [vmem] * 4,
        out_specs=vmem,
        scratch_shapes=[
            pltpu.VMEM((HEAD + ROWS, model), BF16),
            pltpu.VMEM((model, 2 * width), BF16),
            pltpu.VMEM((model, width), BF16),
            pltpu.VMEM((8 * width, w_output.shape[1]), BF16),
            pltpu.VMEM((HEAD + ROWS, 2 * width), F32),
            pltpu.VMEM((HEAD + ROWS, width), F32),
            pltpu.VMEM((2 * ROWS, 128), F32),
            pltpu.VMEM((2 * ROWS, 128), F32),
            pltpu.VMEM((2 * MODES, 8, 128), F32),
            pltpu.VMEM((MODES, width), F32),
            pltpu.VMEM((MODES, width), F32),
            pltpu.VMEM((4, MODES, width), F32),
            pltpu.VMEM((4, MODES, width), F32),
            pltpu.VMEM((16, ROWS, 128), BF16),
            dma((3, NSEM)), dma((3, NSEM)),
            dma((7,)), dma((7,)),
            dma((2, 9)), dma((2, 9)),
            dma((4,)), dma((2,)),
        ],
        compiler_params=pltpu.CompilerParams(
            collective_id=0, has_side_effects=True, vmem_limit_bytes=56 * 1024 * 1024),
        cost_estimate=pl.CostEstimate(flops=2 * ROWS * model * 4 * width, bytes_accessed=2 * ROWS * model, transcendentals=0),
    )(tokens, w_keyval.reshape(depth, 2 * width), w_query, w_output, short_taps, skip_gain[None, :],
      decay_rates.T, residues.T)


def solution(mesh):
    return jax.shard_map(
        shards,
        mesh=mesh,
        in_specs=(
            P("seq", None),
            P("seq", "chan"),
            P("seq", None, "chan"),
            P(None, None, "chan"),
            P("chan"),
            P("chan", None),
            P("chan", None),
            P("seq", "chan"),
        ),
        out_specs=P("seq", "chan"),
        check_vma=False,
    )
```

time: 392 us -> 122 us (0.31)
  the two profiles are of different devices: /device:TPU:1 before, /device:TPU:34 now
where the time goes in v1:
time: 122 us
  Pallas kernels  117 us (96%)
  local copies, waits for them, and re-layouts  4.15 us (3%)
    pallas_call x1, Pallas kernels, shards(): pl.pallas_call(kernel, out_shape=jax.ShapeDtypeStruct((ROWS, w_output.sha...  117 us
    unnamed x2, local copies, waits for them, and re-layouts  4.15 us

profile of v1, /device:TPU:34, one launch (start us, length us, event | category | flops | bytes accessed | tf_op | source)
XLA Modules:
  0.0 121.6 jit_solution(17957403866454642241)
XLA Ops:
  0.0 1.7 %copy.9 = bf16[32,8,2,256]{3,1,2,0:T(8,128)(2,1)} copy(bf16[32,8,2,256]{3,2,1,0:T(2,128)(2,1)} %bitcast.5) | data formatting | bytes 524288
  1.7 117.4 %shard_map.82 = bf16[640,1024]{1,0:T(8,128)(2,1)} custom-call(bf16[640,8192]{1,0:T(8,128)(2,1)} %tok.1, bf16[256,512]{1,0:T(8,128)(2,1)} %bitcast.6, bf16[256,256]{1,0:T(8,128)(2,1)} %wq_in.1, bf16[64,1024]{1,0:T(8,128)(2,1)} %wo_in.1, f32[3,3,256]{2,1,0:T(4,128)} %taps.1, f32[1,256]{1,0:T(1,128)} %bitcast.9, f32[16,256]{1,0:T(8,128)} %bitcast.7, ...), custom_call_target="tpu_custom_call" | custom-call | flops 10737418240 | bytes 10485760 | tf_op jit(solution)/shard_map/pallas_call | solution.py:412
  119.1 2.5 %copy.11 = bf16[640,1024]{1,0:T(8,128)(2,1)} copy(bf16[640,1024]{1,0:T(8,128)(2,1)} %shard_map.82) | data formatting | bytes 2621440

commit v2 on v0

v2 whole, which is shorter than its diff:
```python
import functools

import jax
import jax.numpy as jnp
from jax import lax
from jax.experimental import pallas as pl
from jax.experimental.pallas import tpu as pltpu
from jax.sharding import PartitionSpec as P

MESH = pl.DeviceIdType.MESH
F32 = jnp.float32
BF16 = jnp.bfloat16
MODES = 16
ROWS = 640
SUB = ROWS // 8
HEAD = 16
CUT = 208
ORDER = (
    "0.T", "0.S", "2.T", "1.T", "0.X1", "3.T", "2.S", "0.Z2", "0.Z1", "2.X1", "0.X2", "2.Z1", "2.Z2", "1.S", "1.X2",
    "0.B0+", "E", "0.A1-", "0.D10", "0.Z3", "2.X2", "1.X1", "0.B1-", "0.A0-", "0.X3", "0.A0+", "2.A0+", "0.A1+",
    "1.Z1", "0.B1+", "0.B0-", "1.Z2", "0.A2-", "0.D11", "0.M0", "1.X3", "0.B2-", "2.A1-", "2.Z3", "0.B2+", "1.A0-",
    "0.A2+", "0.D01", "0.D00", "1.B1-", "2.X3", "3.S", "3.X2", "1.B1+", "0.D21", "2.M0", "3.X1", "1.Z3", "0.D02",
    "1.A1+", "0.D12", "2.B0+", "1.A0+", "2.A1+", "1.B0+", "2.B1-", "1.B0-", "2.B1+", "0.D20", "2.A2+", "0.M1",
    "2.D11", "2.A0-", "2.B2+", "4.T", "1.D00", "1.A1-", "0.D22", "1.M0", "2.D01", "2.B0-", "1.D11", "0.M3", "1.B2+",
    "1.D01", "1.B2-", "2.B2-", "1.A2+", "4.S", "0.M2", "1.D21", "1.A2-", "1.D10", "C0", "2.A2-", "3.B0+", "1.D20",
    "3.B1-", "2.D00", "2.D21", "1.M1", "2.D10", "2.D20", "3.B0-", "3.X3", "E10", "3.Z1", "1.M3", "1.D02", "3.B1+",
    "3.Z2", "2.D12", "1.D22", "2.M1", "1.D12", "E20", "4.X2", "4.X1", "3.A0+", "2.M3", "2.D22", "4.Z2", "1.M2",
    "2.D02", "4.Z1", "C1", "3.Z3", "E30", "2.M2", "GT00", "E11", "3.B2-", "4.B0+", "3.A0-", "3.D01", "3.A1-", "3.D00",
    "4.A1+", "3.A1+", "4.B1+", "GT01", "3.A2-", "3.D10", "3.D20", "3.A2+", "3.B2+", "4.A0-", "4.A0+", "3.M0", "4.Z3",
    "GL00", "3.D21", "GY000-", "4.B0-", "3.D11", "E21", "GY000+", "3.D02", "3.D22", "3.D12", "3.M3", "GL01", "4.X3",
    "3.M1", "4.A1-", "3.M2", "GY001+", "GY010-", "GY001-", "GY010+", "E31", "4.D00", "GT10", "GT11", "GL10", "GL11",
    "GY100-", "GY100+", "4.D10", "4.A2+", "4.B1-", "4.A2-", "4.B2-", "4.B2+", "4.D02", "GY011-", "GY011+", "4.D12",
    "GY101-", "GY110-", "GY101+", "4.D20", "4.D11", "4.D01", "4.D22", "GY110+", "GY111-", "GY111+", "4.D21", "OUT0",
    "OUT1",
)


def wrap(value, count):
    return lax.rem(value, count)


def kernel(tok, wkv_in, wq_in, wo_in, taps_in, skip_in, rates_in, resid_in, out,
           x_all, wa0, wa1, wq0, wq1, wo, acc0, acc1, acc_q, mkv, conv, scan, e_own, e_sib, c_x, r_z, gate, acc_o, ends,
           taps, skip, rates, resid, raw,
           send, recv, esend, erecv, gsend, grecv, lsem, tsem):
    seq, chan = lax.axis_index("seq"), lax.axis_index("chan")
    core, xx, zh = lax.rem(seq, 2), lax.rem(seq // 2, 4), seq // 8
    yy, zl = chan // 2, lax.rem(chan, 2)

    def at(z, x, k):
        return (wrap(z, 4) * 4 + wrap(x, 4)) * 2 + k

    def cat(y, l):
        return wrap(y, 4) * 2 + l

    sib = at(zh, xx, 1 - core)
    xp, xm, xo = at(zh, xx + 1, core), at(zh, xx + 3, core), at(zh, xx + 2, core)
    zp, zm, zo = at(zh + 1, xx, core), at(zh + 3, xx, core), at(zh + 2, xx, core)
    yp, ym, lp = cat(yy + 1, zl), cat(yy + 3, zl), cat(yy, 1 - zl)
    following, before = wrap(seq + 1, 32), wrap(seq + 31, 32)

    def copy(src, dst, s, r, **to):
        return pltpu.make_async_remote_copy(
            src_ref=src, dst_ref=dst, send_sem=s, recv_sem=r, device_id=to, device_id_type=MESH)

    barrier = pltpu.get_barrier_semaphore()
    for to in (sib, xp, xm, xo, zp, zm, zo, before):
        pl.semaphore_signal(barrier, inc=1, device_id={"seq": to}, device_id_type=MESH)
    for to in (yp, ym, lp):
        pl.semaphore_signal(barrier, inc=1, device_id={"chan": to}, device_id_type=MESH)
    load = pltpu.make_async_copy(tok, x_all.at[pl.ds(HEAD, ROWS), :], lsem.at[1])
    small = [pltpu.make_async_copy(src, dst, lsem.at[6 + i]) for i, (src, dst) in enumerate(
        ((taps_in, taps), (skip_in, skip), (rates_in, rates), (resid_in, resid)))]
    pairs_in = pltpu.make_async_copy(wkv_in, raw, lsem.at[0])
    pairs_in.start()
    load.start()
    for c in small:
        c.start()

    pairs_in.wait()
    apart = jnp.swapaxes(raw[...], 0, 1)
    mine = pl.ds(pl.multiple_of(seq * raw.shape[0], raw.shape[0]), raw.shape[0])
    for l, ref in enumerate((wa0, wa1)):
        for which in range(2):
            ref[mine, which * 128:(which + 1) * 128] = apart[which, :, l * 128:(l + 1) * 128]
    pl.semaphore_wait(barrier, 11)

    class Gather:
        def __init__(self, p, src, buf, cut):
            self.p, self.src, self.buf = p, src, buf
            self.r, self.n = (raw.shape[0], buf.shape[1]) if src is None else src.shape
            self.cut = cut

        def piece(self, z, x, k, part="", half=None, flip=0):
            first = pl.multiple_of(at(z, x, k) * self.r, self.r)
            low, high = {"": (0, self.r), "A": (0, self.cut), "B": (self.cut, self.r)}[part]
            columns = slice(None)
            if half is not None and high - low < 32:
                columns = pl.ds(half * (self.n // 2), self.n // 2)
            elif half is not None:
                units = (high - low) // 16
                middle = low + (units // 2 if flip else units - units // 2) * 16
                low, high = ((low, middle), (middle, high))[half]
            return self.buf.at[pl.ds(pl.multiple_of(first + low, 16), high - low), columns]

        def put(self, ref, i, to, src=None):
            copy(ref if src is None else src, ref, send.at[self.p], recv.at[self.p, i], seq=to).start()

        def got(self, ref, i):
            copy(ref, ref, send.at[self.p], recv.at[self.p, i], seq=sib).wait_recv()

        def pair(self, dz, dx):
            self.put(self.piece(zh + dz, xx + dx, core), 24 + dx, sib)

        def S(self):
            own = self.piece(zh, xx, core)
            self.put(own, 0, zp, self.src)
            self.put(own, 1, zm, self.src)

        def T(self):
            own = self.piece(zh, xx, core)
            self.put(own, 3, xp, self.src)
            self.put(own, 4, xm, self.src)
            self.put(own, 24, sib, self.src)
            self.local = None
            if self.src is not None:
                self.local = pltpu.make_async_copy(self.src, own, lsem.at[self.p])
                self.local.start()

        def ring(self, where, base, plus, minus, d, flip):
            if d == 3:
                self.got(where(3), base)
                self.put(where(3, 0, flip), base + 2, plus)
            elif d == 1:
                self.got(where(1), base + 1)
                self.put(where(1, 1, flip), base + 2, minus)
            else:
                self.got(where(2), base + 2)

        def X(self, i):
            d = (3, 1, 2)[i]
            self.ring(lambda d, h=None, f=0: self.piece(zh, xx + d, core, "", h, f), 3, xp, xm, d, 0)
            part = self.piece(zh, xx + d, core, "B")
            self.put(part, 15 + 3 * i, zp)
            self.put(part, 16 + 3 * i, zm)
            self.pair(0, d)

        def Z(self, j):
            d = (3, 1, 2)[j]
            self.ring(lambda d, h=None, f=0: self.piece(zh + d, xx, core, "", h, f), 0, zp, zm, d, 0)
            part = self.piece(zh + d, xx, core, "A")
            self.put(part, 6 + 3 * j, xp)
            self.put(part, 7 + 3 * j, xm)
            self.pair(d, 0)

        def A(self, j, d):
            dz = (3, 1, 2)[j]
            self.ring(lambda d, h=None, f=0: self.piece(zh + dz, xx + d, core, "A", h, f),
                      6 + 3 * j, xp, xm, d, (j + self.p) % 2)

        def B(self, i, d):
            dx = (3, 1, 2)[i]
            self.ring(lambda d, h=None, f=0: self.piece(zh + d, xx + dx, core, "B", h, f),
                      15 + 3 * i, zp, zm, d, (i + self.p) % 2)

        def D(self, j, i):
            dz, dx = (3, 1, 2)[j], (3, 1, 2)[i]
            if dx == 2:
                self.A(j, 2)
            if dz == 2:
                self.B(i, 2)
            self.pair(dz, dx)

        def others(self, dx):
            self.got(self.buf.at[pl.ds(0, 4 * self.r), :], 24 + dx)

        def drain(self):
            ref = self.buf.at[pl.ds(0, 31 * self.r), :]
            copy(ref, ref, send.at[self.p], recv.at[self.p, 0], seq=sib).wait_send()

    cut = wa0.shape[0] // 32 * CUT // 256
    gathers = [
        Gather(0, None, wa0, cut),
        Gather(1, None, wa1, cut),
        Gather(2, wq_in.at[:, pl.ds(0, 128)], wq0, cut),
        Gather(3, wq_in.at[:, pl.ds(128, 128)], wq1, cut),
        Gather(4, wo_in, wo, wo_in.shape[0] // 4 * 3),
    ]
    started = []
    sums = [(acc0, 0), (acc1, 0), (acc_q, 0), (acc_q, 128)]

    def multiply(p, dx):
        g = gathers[p]
        acc, low = sums[p]
        if not started:
            started.append(True)
            take_ends()
        if dx == 0:
            if g.local is not None:
                g.local.wait()
        g.others(dx)

        @pl.loop(0, 4)
        def _(dz):
            first = pl.multiple_of(at(zh + dz, xx + dx, 0) * g.r, 2 * g.r)
            columns = pl.ds(first, 2 * g.r)
            acc[:, low:low + g.n] += jnp.dot(x_all[:, columns], g.buf[columns, :], preferred_element_type=F32)

    def short(acc, cols, which, lanes, i):
        v = acc[pl.ds(pl.multiple_of(i * SUB + HEAD - 8, 8), SUB + 8), cols]
        return (taps[0, which:which + 1, lanes] * v[8:] + taps[1, which:which + 1, lanes] * v[7:-1]
                + taps[2, which:which + 1, lanes] * v[6:-2])

    rank8 = lax.broadcasted_iota(jnp.int32, (8, 128), 0)

    def wide(row):
        return jnp.broadcast_to(row, (8, 128))

    def total(terms):
        while len(terms) > 1:
            terms = [p + q for p, q in zip(terms[::2], terms[1::2])]
        return terms[0]

    def eput(src, dst, l, i, to):
        copy(src, dst, esend.at[l], erecv.at[l, i], seq=to).start()

    def egot(ref, l, i):
        copy(ref, ref, esend.at[l], erecv.at[l, i], seq=sib).wait_recv()

    def states(l):
        lanes = slice(l * 128, (l + 1) * 128)
        acc = sums[l][0]
        acc[0:HEAD, :] = jnp.where(seq == 0, 0.0, acc[0:HEAD, :])

        @pl.loop(0, 8)
        def _(i):
            key = short(acc, slice(0, 128), 1, lanes, i)
            value = short(acc, slice(128, 256), 2, lanes, i)
            mkv[pl.ds(pl.multiple_of(l * ROWS + i * SUB, 8), SUB), :] = key * value

        a = [wide(jnp.exp(-rates[m:m + 1, lanes])) for m in range(MODES)]
        r = [wide(resid[m:m + 1, lanes]) for m in range(MODES)]

        def step(t, hs):
            v = mkv[pl.ds(l * ROWS + t, 8, stride=SUB), :]
            hs = [a[m] * hs[m] + v for m in range(MODES)]
            conv[pl.ds(l * ROWS + t, 8, stride=SUB), :] = total([r[m] * hs[m] for m in range(MODES)])
            return tuple(hs)

        hs = lax.fori_loop(0, SUB, step, (jnp.zeros((8, 128), F32),) * MODES)
        for m in range(MODES):
            v = hs[m]
            for d in (1, 2, 4):
                factor = wide(jnp.exp(-rates[m:m + 1, lanes] * float(SUB * d)))
                v = v + jnp.where(rank8 >= d, factor * pltpu.roll(v, d, 0), 0.0)
            scan[l * MODES + m] = v
            e_own[l, m:m + 1, :] = v[7:8, :]
        eput(e_own.at[l], e_sib.at[l], l, 0, sib)

    def pairs(l):
        lam = rates[:, l * 128:(l + 1) * 128]
        e0 = jnp.where(core == 0, e_own[l], e_sib[l])
        e1 = jnp.where(core == 0, e_sib[l], e_own[l])
        return lam, jnp.exp(-lam * float(ROWS)), e0, e1

    def chip_state(l):
        egot(e_sib.at[l], l, 0)
        lam, step1, e0, e1 = pairs(l)
        c_x[l, xx] = step1 * e0 + e1
        mine = c_x.at[l, xx]
        for to in (xp, xm, xo):
            eput(mine, mine, l, 1, to)

    def row_state(l):
        lam = rates[:, l * 128:(l + 1) * 128]
        egot(c_x.at[l, pl.ds(0, 3)], l, 1)
        row = c_x[l, 3]
        for k in range(3):
            row = row + jnp.exp(-lam * float(2 * ROWS * (3 - k))) * c_x[l, k]
        r_z[l, zh] = row
        mine = r_z.at[l, zh]
        for to in (zp, zm, zo):
            eput(mine, mine, l, 2, to)

    def enter(l):
        lanes = slice(l * 128, (l + 1) * 128)
        lam, step1, e0, e1 = pairs(l)
        egot(r_z.at[l, pl.ds(0, 3)], l, 2)
        state = jnp.zeros_like(lam)
        for k in range(3):
            gap = jnp.maximum(zh - 1 - k, 0).astype(F32) * float(8 * ROWS)
            state = state + jnp.where(k < zh, jnp.exp(-lam * gap) * r_z[l, k], 0.0)
        state = jnp.exp(-lam * (xx.astype(F32) * float(2 * ROWS))) * state
        for k in range(3):
            gap = jnp.maximum(xx - 1 - k, 0).astype(F32) * float(2 * ROWS)
            state = state + jnp.where(k < xx, jnp.exp(-lam * gap) * c_x[l, k], 0.0)
        state = jnp.where(core == 0, state, e0 + step1 * state)

        a = [wide(jnp.exp(-rates[m:m + 1, lanes])) for m in range(MODES)]
        gs = []
        for m in range(MODES):
            rate = wide(rates[m:m + 1, lanes])
            first = jnp.where(rank8 >= 1, pltpu.roll(scan[l * MODES + m], 1, 0), 0.0)
            first = first + jnp.exp(-rate * (rank8.astype(F32) * float(SUB))) * wide(state[m:m + 1, :])
            gs.append(wide(resid[m:m + 1, lanes]) * a[m] * first)
        direct = wide(skip[0:1, lanes])

        def step(t, gs):
            place = pl.ds(l * ROWS + t, 8, stride=SUB)
            conv[place, :] = conv[place, :] + total(list(gs)) + direct * mkv[place, :]
            return tuple(a[m] * gs[m] for m in range(MODES))

        lax.fori_loop(0, SUB, step, tuple(gs))

    def gref(c, l, q, half=None):
        rows = ROWS // 2 if half is None else ROWS // 4
        return gate.at[c * 2 + l, pl.ds(q * (ROWS // 2) + (half or 0) * rows, rows), :]

    def gput(ref, l, q, i, to):
        copy(ref, ref, gsend.at[l], grecv.at[l, q, i], chan=to).start()

    def ggot(ref, l, q, i):
        copy(ref, ref, gsend.at[l], grecv.at[l, q, i], chan=lp).wait_recv()

    def gating(l, q):
        lanes = slice(l * 128, (l + 1) * 128)
        if q == 0:
            acc_q[0:HEAD, lanes] = jnp.where(seq == 0, 0.0, acc_q[0:HEAD, lanes])
        mine = gate.at[chan * 2 + l]

        @pl.loop(4 * q, 4 * q + 4)
        def _(i):
            query = short(acc_q, lanes, 0, lanes, i)
            done = query * conv[pl.ds(pl.multiple_of(l * ROWS + i * SUB, 8), SUB), :]
            mine[pl.ds(pl.multiple_of(i * SUB, 16), SUB), :] = done.astype(BF16)

        ref = gref(chan, l, q)
        gput(ref, l, q, 0, lp)
        gput(ref, l, q, 1, yp)
        gput(ref, l, q, 2, ym)

    def gate_pair(l, q):
        ref = gref(lp, l, q)
        ggot(ref, l, q, 0)
        gput(ref, l, q, 3, yp)
        gput(ref, l, q, 4, ym)

    def gate_ring(l, q, j, d):
        side = zl if j == 0 else 1 - zl
        ref = gref(cat(yy + d, side), l, q)
        if d == 3:
            ggot(ref, l, q, 1 + 2 * j)
            gput(gref(cat(yy + 3, side), l, q, 0), l, q, 5 + j, yp)
        elif d == 1:
            ggot(ref, l, q, 2 + 2 * j)
            gput(gref(cat(yy + 1, side), l, q, 1), l, q, 5 + j, ym)
        else:
            ggot(ref, l, q, 5 + j)

    def project(l):
        if l == 0:
            for dx in range(4):
                gathers[4].others(dx)
            gathers[4].local.wait()
        for q in range(2):
            for j in range(2):
                gate_ring(l, q, j, 2)

        @pl.loop(0, out.shape[1] // 256)
        def _(n):
            columns = pl.ds(pl.multiple_of(n * 256, 256), 256)
            left = jnp.concatenate([gate[2 * i + l] for i in range(8)], axis=1)
            right = jnp.concatenate([wo[i * 256 + l * 128:i * 256 + l * 128 + 128, columns] for i in range(8)], axis=0)
            part = jnp.dot(left, right, preferred_element_type=F32)
            if l == 0:
                acc_o[:, columns] = part
            else:
                out[:, columns] = (acc_o[:, columns] + part).astype(BF16)

    tail = copy(ends.at[0], ends.at[1], tsem.at[0], tsem.at[1], seq=following)
    parts = x_all.shape[1] // 8
    rank16 = lax.broadcasted_iota(jnp.int32, (HEAD, parts), 0)

    def send_ends():
        load.wait()
        for c in small:
            c.wait()
        packed = jnp.zeros((HEAD, parts), F32)
        for i in range(8):
            rows = x_all[ROWS:ROWS + HEAD, i * parts:(i + 1) * parts].astype(F32)
            packed = jnp.where(rank16 // 2 == i, pltpu.roll(rows, (2 * i + 2) % HEAD, 0), packed)
        ends[0] = packed.astype(BF16)
        tail.start()

    def take_ends():
        tail.wait_recv()
        packed = ends[1].astype(F32)
        for i in range(8):
            rows = packed if i == 7 else pltpu.roll(packed, HEAD - 2 - 2 * i, 0)
            x_all[0:HEAD, i * parts:(i + 1) * parts] = rows.astype(BF16)

    acc0[...] = jnp.zeros_like(acc0)
    acc1[...] = jnp.zeros_like(acc1)
    acc_q[...] = jnp.zeros_like(acc_q)

    actions = {"E": send_ends, "C": states, "E1": chip_state, "E2": row_state, "E3": enter,
               "GT": gating, "GL": gate_pair, "OUT": project}
    for name in ORDER:
        if "." not in name:
            if name[:2] == "GY":
                gate_ring(int(name[2]), int(name[3]), int(name[4]), 3 if name[5] == "-" else 1)
            else:
                what = name.rstrip("01")
                if name[:2] in ("E1", "E2", "E3"):
                    what = name[:2]
                actions[what](*[int(c) for c in name[len(what):]])
            continue
        g, what = gathers[int(name[0])], name[2:]
        kind = what[0]
        if kind == "M":
            multiply(g.p, int(what[1]))
        elif kind in "ST":
            getattr(g, kind)()
        elif kind in "XZ":
            getattr(g, kind)(int(what[1]) - 1)
        elif kind == "D":
            g.D(int(what[1]), int(what[2]))
        else:
            getattr(g, kind)(int(what[1]), 3 if what[2] == "-" else 1)

    for g in gathers:
        g.drain()
    tail.wait_send()
    for l in range(2):
        ref = mkv.at[pl.ds(0, 7 * MODES), :]
        copy(ref, ref, esend.at[l], erecv.at[l, 0], seq=sib).wait_send()
        ref = gate.at[pl.ds(0, 7)]
        copy(ref, ref, gsend.at[l], grecv.at[l, 0, 0], chan=lp).wait_send()


def shards(tokens, w_query, w_keyval, short_taps, skip_gain, decay_rates, residues, w_output):
    depth, _, width = w_keyval.shape
    hbm, vmem = pl.BlockSpec(memory_space=pl.ANY), pl.BlockSpec(memory_space=pltpu.VMEM)
    dma = pltpu.SemaphoreType.DMA
    model = tokens.shape[1]
    return pl.pallas_call(
        kernel,
        out_shape=jax.ShapeDtypeStruct((ROWS, w_output.shape[1]), BF16),
        in_specs=[hbm] * 8,
        out_specs=vmem,
        scratch_shapes=[
            pltpu.VMEM((HEAD + ROWS, model), BF16),
            pltpu.VMEM((model, width), BF16),
            pltpu.VMEM((model, width), BF16),
            pltpu.VMEM((model, width // 2), BF16),
            pltpu.VMEM((model, width // 2), BF16),
            pltpu.VMEM((8 * width, w_output.shape[1]), BF16),
            pltpu.VMEM((HEAD + ROWS, width), F32),
            pltpu.VMEM((HEAD + ROWS, width), F32),
            pltpu.VMEM((HEAD + ROWS, width), F32),
            pltpu.VMEM((2 * ROWS, 128), F32),
            pltpu.VMEM((2 * ROWS, 128), F32),
            pltpu.VMEM((2 * MODES, 8, 128), F32),
            pltpu.VMEM((2, MODES, 128), F32),
            pltpu.VMEM((2, MODES, 128), F32),
            pltpu.VMEM((2, 4, MODES, 128), F32),
            pltpu.VMEM((2, 4, MODES, 128), F32),
            pltpu.VMEM((16, ROWS, 128), BF16),
            pltpu.VMEM((ROWS, w_output.shape[1]), F32),
            pltpu.VMEM((2, HEAD, model // 8), BF16),
            pltpu.VMEM((3, 3, width), F32),
            pltpu.VMEM((1, width), F32),
            pltpu.VMEM((MODES, width), F32),
            pltpu.VMEM((MODES, width), F32),
            pltpu.VMEM((depth, 2, width), BF16),
            dma((5,)), dma((5, 28)),
            dma((2,)), dma((2, 3)),
            dma((2,)), dma((2, 2, 7)),
            dma((10,)), dma((2,)),
        ],
        compiler_params=pltpu.CompilerParams(
            collective_id=0, has_side_effects=True, vmem_limit_bytes=56 * 1024 * 1024),
        cost_estimate=pl.CostEstimate(flops=2 * ROWS * model * 4 * width, bytes_accessed=2 * ROWS * model, transcendentals=0),
    )(tokens, w_keyval, w_query, w_output, short_taps, skip_gain[None, :],
      decay_rates.T, residues.T)


def solution(mesh):
    return jax.shard_map(
        shards,
        mesh=mesh,
        in_specs=(
            P("seq", None),
            P("seq", "chan"),
            P("seq", None, "chan"),
            P(None, None, "chan"),
            P("chan"),
            P("chan", None),
            P("chan", None),
            P("seq", "chan"),
        ),
        out_specs=P("seq", "chan"),
        check_vma=False,
    )
```

time: 392 us -> 99.7 us (0.25)
  waiting for transfers between devices: 208 us -> 0 us
  Pallas kernels: 0 us -> 97.1 us
  local copies, waits for them, and re-layouts: 63.6 us -> 2.47 us
  matrix products: 57.6 us -> 0 us
  blocking collectives: 28.3 us -> 0 us
  starting transfers between devices: 16.7 us -> 0 us
  between operations: 13.3 us -> 0.01 us
    all_gather x4 -> x0, waiting for transfers between devices: 201 us -> none  [the longest x1 74.3 us: shards(): lax.all_gather(w_keyval, 'seq', axis=0, tiled=True)]
    pallas_call x0 -> x1, Pallas kernels: none -> 97.1 us  [shards(): pl.pallas_call(kernel, out_shape=jax.ShapeDtypeStruct((ROWS, w_output.sha...]
    gather x2 -> x0, local copies, waits for them, and re-layouts: 60.4 us -> none  [modal_block(): toeplitz = jnp.where(lagged >= 0, impulse[:, np.maximum(lagged, 0)], 0.0)]
    dot_general x7 -> x0, matrix products: 57.6 us -> none  [the longest x2 26.3 us: add_projection(): jnp.einsum('dpc,td->pct', portion, tokens, preferred_element_type=jnp.flo...]
    all_to_all x1 -> x0, blocking collectives: 28.3 us -> none  [long_conv(): lax.all_to_all(result, 'seq', split_axis=1, concat_axis=0, tiled=True)]
    all_to_all x1 -> x0, starting transfers between devices: 13.7 us -> none  [long_conv(): lax.all_to_all(mixed_kv, 'seq', split_axis=0, concat_axis=1, tiled=True)]
    ppermute x1 -> x0, waiting for transfers between devices: 5.47 us -> none  [shifted(): lax.ppermute(value, axis, [(source, source + steps) for source in range(i...]
  transfers between devices with their start and end apart: 6 -> 0, of which waited for: 4 -> 0; matrix products, arithmetic and copies ran while one was open for 30% -> 0% of each run, Pallas kernels for 0% -> 0%
where the time goes in v2:
time: 99.7 us; the launch traced here: 99.6 us
  Pallas kernels  97.1 us (97%)
  local copies, waits for them, and re-layouts  2.47 us (2%)
    pallas_call x1, Pallas kernels, shards(): pl.pallas_call(kernel, out_shape=jax.ShapeDtypeStruct((ROWS, w_output.sha...  97.1 us
    unnamed x1, local copies, waits for them, and re-layouts  2.47 us

profile of v2, /device:TPU:1, one launch (start us, length us, event | category | flops | bytes accessed | tf_op | source)
XLA Modules:
  0.0 99.6 jit_solution(7577234104790331657)
XLA Ops:
  0.0 97.1 %shard_map.82 = bf16[640,1024]{1,0:T(8,128)(2,1)} custom-call(bf16[640,8192]{1,0:T(8,128)(2,1)} %tok.1, bf16[256,2,256]{2,1,0:T(2,128)(2,1)} %wkv_in.1, bf16[256,256]{1,0:T(8,128)(2,1)} %wq_in.1, bf16[64,1024]{1,0:T(8,128)(2,1)} %wo_in.1, f32[3,3,256]{2,1,0:T(4,128)} %taps_in.1, f32[1,256]{1,0:T(1,128)} %bitcast.5, f32[16,256]{1,0:T(8,128)} %bitcast.3, ...), custom_call_target="tpu_custom_call" | custom-call | flops 10737418240 | bytes 10485760 | tf_op jit(solution)/shard_map/pallas_call | solution.py:446
  97.1 2.5 %copy.10 = bf16[640,1024]{1,0:T(8,128)(2,1)} copy(bf16[640,1024]{1,0:T(8,128)(2,1)} %shard_map.82) | data formatting | bytes 2621440

commit v3 on v2

--- a/solution.py
+++ b/solution.py
@@ -16,21 +16,21 @@
 HEAD = 16
 CUT = 208
 ORDER = (
-    "0.T", "0.S", "2.T", "1.T", "0.X1", "3.T", "2.S", "0.Z2", "0.Z1", "2.X1", "0.X2", "2.Z1", "2.Z2", "1.S", "1.X2",
-    "0.B0+", "E", "0.A1-", "0.D10", "0.Z3", "2.X2", "1.X1", "0.B1-", "0.A0-", "0.X3", "0.A0+", "2.A0+", "0.A1+",
-    "1.Z1", "0.B1+", "0.B0-", "1.Z2", "0.A2-", "0.D11", "0.M0", "1.X3", "0.B2-", "2.A1-", "2.Z3", "0.B2+", "1.A0-",
-    "0.A2+", "0.D01", "0.D00", "1.B1-", "2.X3", "3.S", "3.X2", "1.B1+", "0.D21", "2.M0", "3.X1", "1.Z3", "0.D02",
-    "1.A1+", "0.D12", "2.B0+", "1.A0+", "2.A1+", "1.B0+", "2.B1-", "1.B0-", "2.B1+", "0.D20", "2.A2+", "0.M1",
-    "2.D11", "2.A0-", "2.B2+", "4.T", "1.D00", "1.A1-", "0.D22", "1.M0", "2.D01", "2.B0-", "1.D11", "0.M3", "1.B2+",
-    "1.D01", "1.B2-", "2.B2-", "1.A2+", "4.S", "0.M2", "1.D21", "1.A2-", "1.D10", "C0", "2.A2-", "3.B0+", "1.D20",
-    "3.B1-", "2.D00", "2.D21", "1.M1", "2.D10", "2.D20", "3.B0-", "3.X3", "E10", "3.Z1", "1.M3", "1.D02", "3.B1+",
-    "3.Z2", "2.D12", "1.D22", "2.M1", "1.D12", "E20", "4.X2", "4.X1", "3.A0+", "2.M3", "2.D22", "4.Z2", "1.M2",
-    "2.D02", "4.Z1", "C1", "3.Z3", "E30", "2.M2", "GT00", "E11", "3.B2-", "4.B0+", "3.A0-", "3.D01", "3.A1-", "3.D00",
-    "4.A1+", "3.A1+", "4.B1+", "GT01", "3.A2-", "3.D10", "3.D20", "3.A2+", "3.B2+", "4.A0-", "4.A0+", "3.M0", "4.Z3",
-    "GL00", "3.D21", "GY000-", "4.B0-", "3.D11", "E21", "GY000+", "3.D02", "3.D22", "3.D12", "3.M3", "GL01", "4.X3",
-    "3.M1", "4.A1-", "3.M2", "GY001+", "GY010-", "GY001-", "GY010+", "E31", "4.D00", "GT10", "GT11", "GL10", "GL11",
-    "GY100-", "GY100+", "4.D10", "4.A2+", "4.B1-", "4.A2-", "4.B2-", "4.B2+", "4.D02", "GY011-", "GY011+", "4.D12",
-    "GY101-", "GY110-", "GY101+", "4.D20", "4.D11", "4.D01", "4.D22", "GY110+", "GY111-", "GY111+", "4.D21", "OUT0",
+    "0.T", "0.S", "2.T", "1.T", "2.S", "0.X2", "3.T", "2.X2", "0.X1", "2.X1", "0.Z2", "0.Z1", "0.X3", "2.Z1", "2.Z2",
+    "0.B0-", "E", "0.B1+", "0.B0+", "0.B1-", "2.X3", "1.S", "2.B1+", "0.A1+", "2.B1-", "1.X2", "2.B0-", "0.D11",
+    "2.B0+", "0.Z3", "0.A1-", "0.A0+", "2.A0+", "2.D01", "0.B2-", "1.X1", "0.B2+", "0.A0-", "0.D00", "2.A0-", "3.S",
+    "3.X1", "2.Z3", "0.D10", "3.X2", "2.D00", "0.D01", "2.A1+", "2.A1-", "0.M0", "2.D11", "0.A2-", "0.D20", "2.M0",
+    "0.A2+", "0.D21", "0.D12", "4.T", "0.M3", "1.Z1", "2.D10", "2.A2+", "2.D21", "0.M1", "0.D02", "1.Z2", "1.B1+",
+    "2.A2-", "1.X3", "2.B2-", "1.B0+", "2.D02", "3.X3", "0.D22", "2.D20", "2.B2+", "1.B1-", "1.B0-", "2.M1", "3.B1+",
+    "3.Z1", "3.Z2", "0.M2", "3.B1-", "3.B0-", "3.B0+", "1.Z3", "C0", "1.A0-", "1.A1+", "1.B2-", "1.B2+", "4.S",
+    "2.D22", "1.A1-", "1.A0+", "3.A1+", "2.D12", "1.M0", "1.D01", "1.D00", "3.B2-", "E10", "1.A2-", "3.A1-", "1.D20",
+    "1.D10", "3.A0-", "1.A2+", "1.D11", "2.M2", "3.Z3", "1.D21", "3.A0+", "2.M3", "1.D12", "1.D02", "1.M3", "1.D22",
+    "E20", "1.M1", "4.X2", "4.Z1", "1.M2", "C1", "E30", "GT00", "3.D01", "3.B2+", "3.A2+", "3.A2-", "3.D21", "3.D20",
+    "3.D11", "E11", "3.D00", "GT01", "3.D10", "4.X1", "3.D12", "3.D02", "3.M0", "3.M1", "E21", "3.D22", "4.Z2",
+    "4.B1-", "GL00", "GY000+", "3.M3", "GL01", "GY000-", "4.A0+", "4.X3", "3.M2", "GY010-", "GY010+", "E31", "GT10",
+    "4.Z3", "4.B0+", "GT11", "4.B2+", "4.B2-", "4.B1+", "4.A1-", "4.B0-", "GY011-", "4.A1+", "4.D01", "GY001+",
+    "4.D10", "GL10", "4.A0-", "4.D11", "4.A2-", "GL11", "4.D00", "4.A2+", "4.D21", "GY001-", "4.D12", "GY011+",
+    "GY110+", "GY100-", "GY100+", "GY110-", "4.D20", "4.D02", "4.D22", "GY101+", "GY101-", "GY111-", "GY111+", "OUT0",
     "OUT1",
 )
 
@@ -41,8 +41,8 @@
 
 def kernel(tok, wkv_in, wq_in, wo_in, taps_in, skip_in, rates_in, resid_in, out,
            x_all, wa0, wa1, wq0, wq1, wo, acc0, acc1, acc_q, mkv, conv, scan, e_own, e_sib, c_x, r_z, gate, acc_o, ends,
-           taps, skip, rates, resid, raw,
-           send, recv, esend, erecv, gsend, grecv, lsem, tsem):
+           taps, skip, rates, resid, raw, held,
+           send, recv, esend, erecv, gsend, grecv, lsem, tsem, osem):
     seq, chan = lax.axis_index("seq"), lax.axis_index("chan")
     core, xx, zh = lax.rem(seq, 2), lax.rem(seq // 2, 4), seq // 8
     yy, zl = chan // 2, lax.rem(chan, 2)
@@ -200,11 +200,12 @@
                 g.local.wait()
         g.others(dx)
 
-        @pl.loop(0, 4)
+        @pl.loop(0, 4, step=2)
         def _(dz):
-            first = pl.multiple_of(at(zh + dz, xx + dx, 0) * g.r, 2 * g.r)
-            columns = pl.ds(first, 2 * g.r)
-            acc[:, low:low + g.n] += jnp.dot(x_all[:, columns], g.buf[columns, :], preferred_element_type=F32)
+            where = [pl.ds(pl.multiple_of(at(zh + dz + i, xx + dx, 0) * g.r, 2 * g.r), 2 * g.r) for i in range(2)]
+            left = jnp.concatenate([x_all[:, w] for w in where], axis=1)
+            right = jnp.concatenate([g.buf[w, :] for w in where], axis=0)
+            acc[:, low:low + g.n] += jnp.dot(left, right, preferred_element_type=F32)
 
     def short(acc, cols, which, lanes, i):
         v = acc[pl.ds(pl.multiple_of(i * SUB + HEAD - 8, 8), SUB + 8), cols]
@@ -375,7 +376,8 @@
             if l == 0:
                 acc_o[:, columns] = part
             else:
-                out[:, columns] = (acc_o[:, columns] + part).astype(BF16)
+                held[:, columns] = (acc_o[:, columns] + part).astype(BF16)
+                pltpu.make_async_copy(held.at[:, columns], out.at[:, columns], osem.at[n]).start()
 
     tail = copy(ends.at[0], ends.at[1], tsem.at[0], tsem.at[1], seq=following)
     parts = x_all.shape[1] // 8
@@ -431,6 +433,12 @@
     for g in gathers:
         g.drain()
     tail.wait_send()
+
+    @pl.loop(0, out.shape[1] // 256)
+    def _(n):
+        columns = pl.ds(pl.multiple_of(n * 256, 256), 256)
+        pltpu.make_async_copy(held.at[:, columns], out.at[:, columns], osem.at[n]).wait()
+
     for l in range(2):
         ref = mkv.at[pl.ds(0, 7 * MODES), :]
         copy(ref, ref, esend.at[l], erecv.at[l, 0], seq=sib).wait_send()
@@ -440,14 +448,14 @@
 
 def shards(tokens, w_query, w_keyval, short_taps, skip_gain, decay_rates, residues, w_output):
     depth, _, width = w_keyval.shape
-    hbm, vmem = pl.BlockSpec(memory_space=pl.ANY), pl.BlockSpec(memory_space=pltpu.VMEM)
+    hbm = pl.BlockSpec(memory_space=pl.ANY)
     dma = pltpu.SemaphoreType.DMA
     model = tokens.shape[1]
     return pl.pallas_call(
         kernel,
         out_shape=jax.ShapeDtypeStruct((ROWS, w_output.shape[1]), BF16),
         in_specs=[hbm] * 8,
-        out_specs=vmem,
+        out_specs=hbm,
         scratch_shapes=[
             pltpu.VMEM((HEAD + ROWS, model), BF16),
             pltpu.VMEM((model, width), BF16),
@@ -473,10 +481,11 @@
             pltpu.VMEM((MODES, width), F32),
             pltpu.VMEM((MODES, width), F32),
             pltpu.VMEM((depth, 2, width), BF16),
+            pltpu.VMEM((ROWS, w_output.shape[1]), BF16),
             dma((5,)), dma((5, 28)),
             dma((2,)), dma((2, 3)),
             dma((2,)), dma((2, 2, 7)),
-            dma((10,)), dma((2,)),
+            dma((10,)), dma((2,)), dma((4,)),
         ],
         compiler_params=pltpu.CompilerParams(
             collective_id=0, has_side_effects=True, vmem_limit_bytes=56 * 1024 * 1024),

time: 99.7 us -> 96.4 us (0.967)
  Pallas kernels: 97.1 us -> 93.8 us
    pallas_call x1, Pallas kernels: 97.1 us -> 93.8 us  [shards(): pl.pallas_call(kernel, out_shape=jax.ShapeDtypeStruct((ROWS, w_output.sha...]
where the time goes in v3:
time: 96.4 us; the launch traced here: 96.3 us
  Pallas kernels  93.8 us (97%)
  local copies, waits for them, and re-layouts  2.47 us (3%)
    pallas_call x1, Pallas kernels, shards(): pl.pallas_call(kernel, out_shape=jax.ShapeDtypeStruct((ROWS, w_output.sha...  93.8 us
    unnamed x1, local copies, waits for them, and re-layouts  2.47 us

profile of v3, /device:TPU:1, one launch (start us, length us, event | category | flops | bytes accessed | tf_op | source)
XLA Modules:
  0.0 96.3 jit_solution(8358240797296455664)
XLA Ops:
  0.0 93.8 %shard_map.82 = bf16[640,1024]{1,0:T(8,128)(2,1)} custom-call(bf16[640,8192]{1,0:T(8,128)(2,1)} %tok.1, bf16[256,2,256]{2,1,0:T(2,128)(2,1)} %wkv_in.1, bf16[256,256]{1,0:T(8,128)(2,1)} %wq_in.1, bf16[64,1024]{1,0:T(8,128)(2,1)} %wo_in.1, f32[3,3,256]{2,1,0:T(4,128)} %taps_in.1, f32[1,256]{1,0:T(1,128)} %bitcast.5, f32[16,256]{1,0:T(8,128)} %bitcast.3, ...), custom_call_target="tpu_custom_call" | custom-call | flops 10737418240 | bytes 10485760 | tf_op jit(solution)/shard_map/pallas_call | solution.py:454
  93.8 2.5 %copy.10 = bf16[640,1024]{1,0:T(8,128)(2,1)} copy(bf16[640,1024]{1,0:T(8,128)(2,1)} %shard_map.82) | data formatting | bytes 2621440

commit v4 on v3

--- a/solution.py
+++ b/solution.py
@@ -14,24 +14,25 @@
 ROWS = 640
 SUB = ROWS // 8
 HEAD = 16
-CUT = 208
+CUT = 224
+CUT_KV = 224
 ORDER = (
-    "0.T", "0.S", "2.T", "1.T", "2.S", "0.X2", "3.T", "2.X2", "0.X1", "2.X1", "0.Z2", "0.Z1", "0.X3", "2.Z1", "2.Z2",
-    "0.B0-", "E", "0.B1+", "0.B0+", "0.B1-", "2.X3", "1.S", "2.B1+", "0.A1+", "2.B1-", "1.X2", "2.B0-", "0.D11",
-    "2.B0+", "0.Z3", "0.A1-", "0.A0+", "2.A0+", "2.D01", "0.B2-", "1.X1", "0.B2+", "0.A0-", "0.D00", "2.A0-", "3.S",
-    "3.X1", "2.Z3", "0.D10", "3.X2", "2.D00", "0.D01", "2.A1+", "2.A1-", "0.M0", "2.D11", "0.A2-", "0.D20", "2.M0",
-    "0.A2+", "0.D21", "0.D12", "4.T", "0.M3", "1.Z1", "2.D10", "2.A2+", "2.D21", "0.M1", "0.D02", "1.Z2", "1.B1+",
-    "2.A2-", "1.X3", "2.B2-", "1.B0+", "2.D02", "3.X3", "0.D22", "2.D20", "2.B2+", "1.B1-", "1.B0-", "2.M1", "3.B1+",
-    "3.Z1", "3.Z2", "0.M2", "3.B1-", "3.B0-", "3.B0+", "1.Z3", "C0", "1.A0-", "1.A1+", "1.B2-", "1.B2+", "4.S",
-    "2.D22", "1.A1-", "1.A0+", "3.A1+", "2.D12", "1.M0", "1.D01", "1.D00", "3.B2-", "E10", "1.A2-", "3.A1-", "1.D20",
-    "1.D10", "3.A0-", "1.A2+", "1.D11", "2.M2", "3.Z3", "1.D21", "3.A0+", "2.M3", "1.D12", "1.D02", "1.M3", "1.D22",
-    "E20", "1.M1", "4.X2", "4.Z1", "1.M2", "C1", "E30", "GT00", "3.D01", "3.B2+", "3.A2+", "3.A2-", "3.D21", "3.D20",
-    "3.D11", "E11", "3.D00", "GT01", "3.D10", "4.X1", "3.D12", "3.D02", "3.M0", "3.M1", "E21", "3.D22", "4.Z2",
-    "4.B1-", "GL00", "GY000+", "3.M3", "GL01", "GY000-", "4.A0+", "4.X3", "3.M2", "GY010-", "GY010+", "E31", "GT10",
-    "4.Z3", "4.B0+", "GT11", "4.B2+", "4.B2-", "4.B1+", "4.A1-", "4.B0-", "GY011-", "4.A1+", "4.D01", "GY001+",
-    "4.D10", "GL10", "4.A0-", "4.D11", "4.A2-", "GL11", "4.D00", "4.A2+", "4.D21", "GY001-", "4.D12", "GY011+",
-    "GY110+", "GY100-", "GY100+", "GY110-", "4.D20", "4.D02", "4.D22", "GY101+", "GY101-", "GY111-", "GY111+", "OUT0",
-    "OUT1",
+    "2.T", "2.S", "3.T", "RL", "0.T", "0.S", "1.T", "2.X2", "2.Z1", "2.Z2", "0.X1", "2.X1", "0.X2", "E", "0.Z2",
+    "0.Z1", "2.Z3", "2.A0-", "2.B1+", "2.A0+", "2.B1-", "2.X3", "2.B0-", "2.A1-", "0.B1+", "0.B1-", "0.X3", "2.B0+",
+    "2.D01", "1.S", "2.M0", "1.X2", "0.Z3", "0.A1-", "0.B0+", "0.A1+", "0.B0-", "2.D10", "2.B2+", "2.A1+", "3.S",
+    "2.D11", "3.X2", "0.D11", "2.B2-", "2.D00", "0.D10", "3.X1", "0.B2-", "0.B2+", "1.X1", "0.A0-", "2.A2+", "2.D02",
+    "2.D21", "0.A0+", "2.A2-", "2.D20", "0.D00", "0.M0", "2.M3", "0.D01", "0.A2+", "0.A2-", "0.D21", "1.Z1", "1.Z2",
+    "0.D20", "2.M1", "0.D12", "3.X3", "1.B1+", "4.T", "0.D02", "0.M1", "0.D22", "1.B1-", "1.X3", "1.B0+", "1.B0-",
+    "2.D12", "4.S", "0.M3", "2.D22", "1.Z3", "0.M2", "C0", "1.A1+", "1.A0+", "3.B1-", "1.A0-", "1.D11", "1.A1-",
+    "2.M2", "3.B2-", "3.B0+", "3.B1+", "1.D10", "1.B2+", "3.B0-", "1.D01", "1.B2-", "1.D00", "E10", "1.A2-", "1.A2+",
+    "1.D21", "3.Z1", "3.Z2", "1.D20", "1.M0", "4.X2", "4.X1", "1.D02", "1.M1", "1.D12", "E20", "1.D22", "3.B2+",
+    "1.M3", "3.Z3", "4.Z1", "3.A1+", "3.D11", "3.A0+", "3.A0-", "3.D01", "1.M2", "C1", "3.A1-", "E30", "GT00",
+    "3.A2-", "3.A2+", "3.D21", "E11", "GT01", "3.M0", "3.D10", "3.D20", "3.D00", "3.D02", "3.M1", "E21", "3.D22",
+    "4.Z2", "3.D12", "GL00", "GY000+", "3.M3", "GL01", "GY000-", "GY010+", "4.X3", "GY010-", "3.M2", "E31", "GT10",
+    "4.Z3", "GT11", "4.B1-", "4.B0-", "4.B1+", "GY001+", "4.B0+", "4.A1+", "4.A0-", "4.A1-", "4.D11", "GY001-",
+    "4.A0+", "4.B2-", "GL10", "4.B2+", "4.D01", "4.A2+", "4.A2-", "GL11", "GY011+", "4.D00", "4.D20", "GY011-",
+    "GY110+", "4.D10", "4.D12", "4.D02", "4.D21", "GY110-", "GY100-", "GY100+", "4.D22", "GY111+", "GY111-", "GY101-",
+    "GY101+", "OUT0", "OUT1",
 )
 
 
@@ -77,12 +78,9 @@
     for c in small:
         c.start()
 
-    pairs_in.wait()
-    apart = jnp.swapaxes(raw[...], 0, 1)
-    mine = pl.ds(pl.multiple_of(seq * raw.shape[0], raw.shape[0]), raw.shape[0])
-    for l, ref in enumerate((wa0, wa1)):
-        for which in range(2):
-            ref[mine, which * 128:(which + 1) * 128] = apart[which, :, l * 128:(l + 1) * 128]
+    acc0[...] = jnp.zeros_like(acc0)
+    acc1[...] = jnp.zeros_like(acc1)
+    acc_q[...] = jnp.zeros_like(acc_q)
     pl.semaphore_wait(barrier, 11)
 
     class Gather:
@@ -178,12 +176,11 @@
             ref = self.buf.at[pl.ds(0, 31 * self.r), :]
             copy(ref, ref, send.at[self.p], recv.at[self.p, 0], seq=sib).wait_send()
 
-    cut = wa0.shape[0] // 32 * CUT // 256
     gathers = [
-        Gather(0, None, wa0, cut),
-        Gather(1, None, wa1, cut),
-        Gather(2, wq_in.at[:, pl.ds(0, 128)], wq0, cut),
-        Gather(3, wq_in.at[:, pl.ds(128, 128)], wq1, cut),
+        Gather(0, None, wa0, CUT_KV),
+        Gather(1, None, wa1, CUT_KV),
+        Gather(2, wq_in.at[:, pl.ds(0, 128)], wq0, CUT),
+        Gather(3, wq_in.at[:, pl.ds(128, 128)], wq1, CUT),
         Gather(4, wo_in, wo, wo_in.shape[0] // 4 * 3),
     ]
     started = []
@@ -383,6 +380,14 @@
     parts = x_all.shape[1] // 8
     rank16 = lax.broadcasted_iota(jnp.int32, (HEAD, parts), 0)
 
+    def rows_apart():
+        pairs_in.wait()
+        apart = jnp.swapaxes(raw[...], 0, 1)
+        mine = pl.ds(pl.multiple_of(seq * raw.shape[0], raw.shape[0]), raw.shape[0])
+        for l, ref in enumerate((wa0, wa1)):
+            for which in range(2):
+                ref[mine, which * 128:(which + 1) * 128] = apart[which, :, l * 128:(l + 1) * 128]
+
     def send_ends():
         load.wait()
         for c in small:
@@ -401,11 +406,8 @@
             rows = packed if i == 7 else pltpu.roll(packed, HEAD - 2 - 2 * i, 0)
             x_all[0:HEAD, i * parts:(i + 1) * parts] = rows.astype(BF16)
 
-    acc0[...] = jnp.zeros_like(acc0)
-    acc1[...] = jnp.zeros_like(acc1)
-    acc_q[...] = jnp.zeros_like(acc_q)
-
-    actions = {"E": send_ends, "C": states, "E1": chip_state, "E2": row_state, "E3": enter,
+
+    actions = {"RL": rows_apart, "E": send_ends, "C": states, "E1": chip_state, "E2": row_state, "E3": enter,
                "GT": gating, "GL": gate_pair, "OUT": project}
     for name in ORDER:
         if "." not in name:

time: 96.4 us -> 94.6 us (0.981)
  Pallas kernels: 93.8 us -> 91.2 us
    pallas_call x1, Pallas kernels: 93.8 us -> 91.2 us  [shards(): pl.pallas_call(kernel, out_shape=jax.ShapeDtypeStruct((ROWS, w_output.sha...]
where the time goes in v4:
time: 94.6 us; the launch traced here: 93.6 us
  Pallas kernels  91.2 us (96%)
  local copies, waits for them, and re-layouts  2.47 us (3%)
    pallas_call x1, Pallas kernels, shards(): pl.pallas_call(kernel, out_shape=jax.ShapeDtypeStruct((ROWS, w_output.sha...  91.2 us
    unnamed x1, local copies, waits for them, and re-layouts  2.47 us

profile of v4, /device:TPU:1, one launch (start us, length us, event | category | flops | bytes accessed | tf_op | source)
XLA Modules:
  0.0 93.6 jit_solution(5872625489999821351)
XLA Ops:
  0.0 91.2 %shard_map.82 = bf16[640,1024]{1,0:T(8,128)(2,1)} custom-call(bf16[640,8192]{1,0:T(8,128)(2,1)} %tok.1, bf16[256,2,256]{2,1,0:T(2,128)(2,1)} %wkv_in.1, bf16[256,256]{1,0:T(8,128)(2,1)} %wq_in.1, bf16[64,1024]{1,0:T(8,128)(2,1)} %wo_in.1, f32[3,3,256]{2,1,0:T(4,128)} %taps_in.1, f32[1,256]{1,0:T(1,128)} %bitcast.5, f32[16,256]{1,0:T(8,128)} %bitcast.3, ...), custom_call_target="tpu_custom_call" | custom-call | flops 10737418240 | bytes 10485760 | tf_op jit(solution)/shard_map/pallas_call | solution.py:456
  91.2 2.5 %copy.10 = bf16[640,1024]{1,0:T(8,128)(2,1)} copy(bf16[640,1024]{1,0:T(8,128)(2,1)} %shard_map.82) | data formatting | bytes 2621440
